TPU v7x, 256 devices: a whole 4x4x8 slice. The times are simulated.
256 devices in a mesh: dp: 2 (over core), seq: 32 (over z, y), head: 4 (over x).
Axes of the slice: x: 4, y: 4, z: 8, core: 2. Of those that a mesh axis runs over, the one named last changes fastest.
Arguments:
- prompt_key_input: bfloat16 [2, 6144, 512], P('dp', 'seq', 'head'), may hold values from -6 to 6
- prompt_value_input: bfloat16 [2, 6144, 512], P('dp', 'seq', 'head'), may hold values from -6 to 6
- resp_queries: bfloat16 [2, 32, 128, 4096], P('dp', 'seq', None, 'head'), may hold values from -6 to 6
- response_key_input: bfloat16 [2, 32, 128, 512], P('dp', 'seq', None, 'head'), may hold values from -6 to 6
- response_value_input: bfloat16 [2, 32, 128, 512], P('dp', 'seq', None, 'head'), may hold values from -6 to 6
- q_gain: float32 [128], replicated, may hold values from 0.5 to 3.5
- k_gain: float32 [128], replicated, may hold values from 0.5 to 3.5
- groups: int32 [2, 32], P('dp', 'seq'), may hold values from 0 to 1, as said below
- lengths: int32 [2, 32], P('dp', 'seq'), may hold values from 32 to 128, as said below
- tiles: int32 [2, 32, 48], P('dp', 'seq'), may hold values 0 or 1
- advantages: float32 [2, 32], P('dp', 'seq'), may hold values from -3 to 3
- upstream: bfloat16 [2, 32, 128, 4096], P('dp', 'seq', None, 'head'), may hold values from -6 to 6
Outputs:
- response_query_gradient: float32 [2, 32, 128, 4096], P('dp', 'seq', 'head')
- response_key_gradient: float32 [2, 32, 128, 512], P('dp', 'seq', None, 'head')
- grad_resp_values: float32 [2, 32, 128, 512], P('dp', 'seq', None, 'head')
- prompt_key_gradient: float32 [2, 6144, 512], P('dp', 'seq', 'head')
- prompt_value_gradient: float32 [2, 6144, 512], P('dp', 'seq', 'head')
- query_gain_gradient: float32 [128], replicated
- grad_k_gain: float32 [128], replicated
Inputs may be any that keep to these rules, and one draw needn't show every extreme that they name: `groups`: each prompt 0 to 1 of a set is named by exactly 16 of its responses. `lengths`: in each set some response has length 128.
All inputs are finite; a program needn't handle non-finite values. No bound on the sum of `tiles` on one device may be relied on, other than what follows from the above.
Results may differ from a plain program's by a relative error of at most 0.008.
The roundings to bfloat16 on the way count: a program that leaves them out, or rounds other values in their place, can miss the bound.
Values may be sent and summed in bfloat16 or wider, within the bound.
No kernel may reach another device: no remote copies, remote signals or barrier semaphores. Data moves between devices by JAX's collectives and lax.ppermute only.
A program may use at most 128 MiB of HBM per device.

v0:
```python
import jax
import jax.numpy as jnp
from jax import lax
from jax.sharding import PartitionSpec as P

TILE = 64


EPSILON = 1e-06
NEGATIVE = -1e30


def head_norm(inputs, gains):
    return inputs * lax.rsqrt(jnp.mean(inputs * inputs, axis=-1, keepdims=True) + EPSILON) * gains


def repeat_mask(tile_row, tile_size):
    return jnp.repeat(tile_row, tile_size, total_repeat_length=tile_row.shape[0] * tile_size) > 0


def raw_scores(query_hat, key_block, score_scale):
    return jnp.dot(query_hat, key_block.T, preferred_element_type=jnp.float32) * score_scale


def stats_core(running, query_hat, key_block, allowed, score_scale):
    row_max, row_sum = running
    scores = raw_scores(query_hat, key_block, score_scale)
    new_max = jnp.maximum(row_max, jnp.max(jnp.where(allowed, scores, NEGATIVE), axis=1))
    terms = jnp.where(allowed, jnp.exp(scores - new_max[:, None]), 0.0)
    return (new_max, row_sum * jnp.exp(row_max - new_max) + jnp.sum(terms, axis=1))


def weights_of(query_hat, key_block, allowed, log_total, score_scale):
    scores = raw_scores(query_hat, key_block, score_scale)
    return jnp.where(allowed, jnp.exp(scores - log_total[:, None]), 0.0)


def values_core(attended, query_hat, key_block, value_block, allowed, log_total, score_scale):
    weights = weights_of(query_hat, key_block, allowed, log_total, score_scale).astype(jnp.bfloat16)
    return attended + jnp.dot(weights, value_block, preferred_element_type=jnp.float32)


def score_grads(
    query_hat, key_block, value_block, allowed, log_total, grad_out, out_dot, score_scale
):
    weights = weights_of(query_hat, key_block, allowed, log_total, score_scale)
    grad_probs = jnp.dot(grad_out, value_block.T, preferred_element_type=jnp.float32)
    return (
        weights.astype(jnp.bfloat16),
        (weights * (grad_probs - out_dot[:, None])).astype(jnp.bfloat16),
    )


def query_core(
    grad_query,
    query_hat,
    key_block,
    value_block,
    allowed,
    log_total,
    grad_out,
    out_dot,
    score_scale,
):
    weights_b, grad_scores = score_grads(
        query_hat, key_block, value_block, allowed, log_total, grad_out, out_dot, score_scale
    )
    return (
        grad_query
        + jnp.dot(grad_scores, key_block, preferred_element_type=jnp.float32) * score_scale
    )


def key_value_core(
    query_hat, key_block, value_block, allowed, log_total, grad_out, out_dot, score_scale
):
    weights_b, grad_scores = score_grads(
        query_hat, key_block, value_block, allowed, log_total, grad_out, out_dot, score_scale
    )
    grad_vals = jnp.dot(weights_b.T, grad_out, preferred_element_type=jnp.float32)
    grad_keys = jnp.dot(grad_scores.T, query_hat, preferred_element_type=jnp.float32) * score_scale
    return jnp.concatenate([grad_keys, grad_vals], axis=1)


def over_blocks(block_step, running, pieces, block_rows):
    row_count = pieces[0].shape[0]
    stacked = tuple(
        (
            shard_rows.reshape((row_count // block_rows, block_rows) + shard_rows.shape[1:])
            for shard_rows in pieces
        )
    )
    firsts = block_rows * jnp.arange(row_count // block_rows, dtype=jnp.int32)

    def over_advance(current, element):
        return (block_step(current, element[1], element[0]), None)

    running, unused = lax.scan(over_advance, running, (firsts, stacked))
    return running


def bypass(current):
    return current


def shards(
    prompt_key_input,
    prompt_value_input,
    resp_queries,
    response_key_input,
    response_value_input,
    q_gain,
    k_gain,
    groups,
    lengths,
    tiles,
    advantages,
    upstream,
):
    head_size = q_gain.shape[0]
    block_rows = prompt_key_input.shape[1]
    resp_len = resp_queries.shape[2]
    group_heads = resp_queries.shape[3] // head_size
    query_count = resp_len * group_heads
    score_scale = head_size ** (-0.5)
    prompt_len = block_rows * max(1, min(16, lax.axis_size("seq") // 2))
    copies = block_rows * lax.axis_size("seq") // prompt_len
    my_group = groups[0, 0]
    resp_length = lengths[0, 0]
    advantage = advantages[0, 0]
    tile_row = tiles[0, 0]
    token_ids = jnp.arange(query_count, dtype=jnp.int32) // group_heads
    query_raw = resp_queries[0, 0].astype(jnp.float32).reshape(resp_len, group_heads, head_size)
    query_full, query_back = jax.vjp(head_norm, query_raw, q_gain)
    query_hat = query_full.astype(jnp.bfloat16).reshape(query_count, head_size)
    unnormed_key = response_key_input[0, 0].astype(jnp.float32)
    key_full, key_back = jax.vjp(head_norm, unnormed_key, k_gain)
    key_hat = key_full.astype(jnp.bfloat16)
    response_value_rows = response_value_input[0, 0]
    unnormed_prompt = prompt_key_input[0].astype(jnp.float32)
    prompt_full, prompt_back = jax.vjp(head_norm, unnormed_prompt, k_gain)
    prompt_hat = prompt_full.astype(jnp.bfloat16)
    prompt_value_rows = prompt_value_input[0]
    upstream_rows = upstream[0, 0].reshape(query_count, head_size)
    causal = jnp.arange(resp_len, dtype=jnp.int32)[None, :] <= token_ids[:, None]
    own_mask = repeat_mask(tile_row, TILE)
    prompt_match = (jnp.arange(copies, dtype=jnp.int32) == my_group)[:, None]
    set_mask = (prompt_match & own_mask[None, :]).reshape(copies * prompt_len)

    def prefix_allowed(first_row, row_count):
        owned = (first_row // prompt_len == my_group) | (
            (first_row + row_count - 1) // prompt_len == my_group
        )
        return (owned, lax.dynamic_slice_in_dim(set_mask, first_row, row_count, 0)[None, :])

    def stats_block(running, pieces, first_row):
        owned, allowed = prefix_allowed(first_row, pieces[0].shape[0])

        def stats_compute(current):
            return stats_core(current, query_hat, pieces[0], allowed, score_scale)

        return lax.cond(owned, stats_compute, bypass, running)

    start_stats = (
        jnp.full((query_count,), NEGATIVE, jnp.float32),
        jnp.zeros((query_count,), jnp.float32),
    )
    stats = over_blocks(
        stats_block,
        start_stats,
        (lax.all_gather(prompt_hat, "seq", axis=0, tiled=True),),
        prompt_len,
    )
    row_max, row_sum = stats_core(stats, query_hat, key_hat, causal, score_scale)
    log_total = row_max + jnp.log(row_sum)

    def values_block(running, pieces, first_row):
        owned, allowed = prefix_allowed(first_row, pieces[0].shape[0])

        def values_compute(current):
            return values_core(
                current, query_hat, pieces[0], pieces[1], allowed, log_total, score_scale
            )

        return lax.cond(owned, values_compute, bypass, running)

    start_out = jnp.zeros((query_count, head_size), jnp.float32)
    attended = over_blocks(
        values_block,
        start_out,
        (
            lax.all_gather(prompt_hat, "seq", axis=0, tiled=True),
            lax.all_gather(prompt_value_rows, "seq", axis=0, tiled=True),
        ),
        prompt_len,
    )
    attended = values_core(
        attended, query_hat, key_hat, response_value_rows, causal, log_total, score_scale
    )
    grad_out = jnp.where(
        (token_ids < resp_length)[:, None], -advantage * upstream_rows.astype(jnp.float32), 0.0
    ).astype(jnp.bfloat16)
    out_dot = jnp.sum(grad_out.astype(jnp.float32) * attended, axis=1)
    weights_b, grad_scores = score_grads(
        query_hat, key_hat, response_value_rows, causal, log_total, grad_out, out_dot, score_scale
    )
    grad_resp_vals = jnp.dot(weights_b.T, grad_out, preferred_element_type=jnp.float32)
    response_key_gradient = (
        jnp.dot(grad_scores.T, query_hat, preferred_element_type=jnp.float32) * score_scale
    )
    local_query = jnp.dot(grad_scores, key_hat, preferred_element_type=jnp.float32) * score_scale

    def query_block(running, pieces, first_row):
        owned, allowed = prefix_allowed(first_row, pieces[0].shape[0])

        def query_compute(current):
            return query_core(
                current,
                query_hat,
                pieces[0],
                pieces[1],
                allowed,
                log_total,
                grad_out,
                out_dot,
                score_scale,
            )

        return lax.cond(owned, query_compute, bypass, running)

    grad_query = over_blocks(
        query_block,
        local_query,
        (
            lax.all_gather(prompt_hat, "seq", axis=0, tiled=True),
            lax.all_gather(prompt_value_rows, "seq", axis=0, tiled=True),
        ),
        prompt_len,
    )
    own_start = lax.axis_index("seq") * block_rows
    own_prompt = own_start // prompt_len
    own_offset = own_start % prompt_len
    all_totals, all_dots = (
        lax.all_gather(log_total[None], "seq", axis=0, tiled=True),
        lax.all_gather(out_dot[None], "seq", axis=0, tiled=True),
    )
    info = jnp.concatenate([my_group[None], tile_row])[None]
    initial_gradients = jnp.zeros((block_rows, 2 * head_size), jnp.float32)
    running = initial_gradients
    pieces = (
        lax.all_gather(query_hat[None], "seq", axis=0, tiled=True),
        lax.all_gather(grad_out[None], "seq", axis=0, tiled=True),
        lax.all_gather(info, "seq", axis=0, tiled=True),
    )

    def take_advance(current, element):
        query_in, grad_in, info_in, total_in, dot_in = element
        own_tiles = lax.dynamic_slice_in_dim(
            repeat_mask(info_in[1:], TILE), own_offset, block_rows, 0
        )[None, :]

        def take_compute(inner):
            return inner + key_value_core(
                query_in,
                prompt_hat,
                prompt_value_rows,
                own_tiles,
                total_in,
                grad_in,
                dot_in,
                score_scale,
            )

        return (lax.cond(info_in[0] == own_prompt, take_compute, bypass, current), None)

    running, unused = lax.scan(
        take_advance, running, (pieces[0], pieces[1], pieces[2], all_totals, all_dots)
    )
    grad_prompt_hat = running[:, :head_size]
    grad_prompt_vals = running[:, head_size:]
    grad_query_raw, gain_query = query_back(grad_query.reshape(resp_len, group_heads, head_size))
    grad_key_raw, response_gain_factor = key_back(response_key_gradient)
    grad_prompt_raw, prompt_gain_factor = prompt_back(grad_prompt_hat)
    gains = lax.psum((gain_query, prompt_gain_factor + response_gain_factor), ("dp", "seq", "head"))
    regrouped = lax.all_to_all(
        grad_query_raw.reshape(1, 1, resp_len, group_heads * head_size).astype(jnp.bfloat16),
        "head",
        split_axis=2,
        concat_axis=3,
        tiled=True,
    ).astype(jnp.float32)
    return (
        regrouped,
        grad_key_raw[None, None],
        grad_resp_vals[None, None],
        grad_prompt_raw[None],
        grad_prompt_vals[None],
        gains[0],
        gains[1],
    )


def solution(mesh):
    placed = (
        P("dp", "seq", "head"),
        P("dp", "seq", "head"),
        P("dp", "seq", None, "head"),
        P("dp", "seq", None, "head"),
        P("dp", "seq", None, "head"),
        P(),
        P(),
        P("dp", "seq"),
        P("dp", "seq"),
        P("dp", "seq", None),
        P("dp", "seq"),
        P("dp", "seq", None, "head"),
    )
    return jax.shard_map(
        shards,
        mesh=mesh,
        in_specs=placed,
        out_specs=(
            P("dp", "seq", "head", None),
            P("dp", "seq", None, "head"),
            P("dp", "seq", None, "head"),
            P("dp", "seq", "head"),
            P("dp", "seq", "head"),
            P(),
            P(),
        ),
        check_vma=False,
    )
```

profile of v0, /device:TPU:6, one launch (start us, length us, event | category | flops | bytes accessed | tf_op | source)
XLA Modules:
  0.0 1071.7 jit_solution(8215483866125135772)
XLA Ops:
  60.8 30.6 %select_compare_fusion = pred[3072]{0:T(1024)(128)(4,1)S(1)} fusion(s32[24,128]{1,0:T(8,128)} %constant.495.clone.1, s32[]{:T(128)} %bitcast.119, s32[]{:T(128)} %bitcast.118, s32[]{:T(128)} %bitcast.117, s32[]{:T(128)} %bitcast.116, s32[]{:T(128)} %bitcast.115, s32[]{:T(128)} %bitcast.114, s32[]{:T(128)} %bitcast.113, s32[]{:T(128)} %bitcast.112, ...), kind=kLoop, calls=%fused_computation.183 | loop fusion | flops 319488 | bytes 15648 | tf_op jit(solution)/shard_map/gt | solution.py:18
  111.9 56.8 %all-gather.15.cloned.1.call-done = bf16[1,6144,128]{2,1,0:T(8,128)(2,1)} async-done(((bf16[1,192,128]{2,1,0:T(8,128)(2,1)}), bf16[1,6144,128]{2,1,0:T(8,128)(2,1)}) %all-gather.15.cloned.1.call-update) | async-done | bytes 1572880 | tf_op jit(solution)/shard_map/all_gather | solution.py:193
  189.4 31.8 %while.78 = (s32[]{:T(128)}, f32[1024,128]{1,0:T(8,128)S(1)}, s32[2]{0:T(128)}, s32[]{:T(128)}, bf16[2,3072,128]{2,1,0:T(8,128)(2,1)}, /*index=5*/bf16[1024,128]...) while((s32[]{:T(128)}, f32[1024,128]{1,0:T(8,128)S(1)}, ...), condition=%wide.region_19.21_spmd.clone, body=%wide.region_16.20_spmd.clone.sunk | while | flops 2435061760 | bytes 35430424 | solution.py:98
  232.1 41.9 %all-gather.2 = f32[32768]{0:T(1024)S(1)} all-gather(f32[1024]{0:T(1024)S(1)} %get-tuple-element.2804), channel_id=4, replica_groups=mesh['dp'=2,'seq'=32,'head'=4] {'seq'}, dimensions={0}, use_global_device_ids=true | all-gather | bytes 135168 | tf_op jit(solution)/shard_map/all_gather | solution.py:244
  274.1 41.7 %all-gather.3 = f32[32768]{0:T(1024)S(1)} all-gather(f32[1024]{0:T(1024)S(1)} %get-tuple-element.2805), channel_id=5, replica_groups=mesh['dp'=2,'seq'=32,'head'=4] {'seq'}, dimensions={0}, use_global_device_ids=true | all-gather | bytes 135168 | tf_op jit(solution)/shard_map/all_gather | solution.py:245
  323.6 42.4 %all-gather.13.cloned.1.call-done = bf16[32,1024,128]{2,1,0:T(8,128)(2,1)} async-done(((bf16[1,1024,128]{2,1,0:T(8,128)(2,1)}), bf16[32,1024,128]{2,1,0:T(8,128)(2,1)}) %all-gather.13.cloned.1.call-update) | async-done | bytes 8388624 | tf_op jit(solution)/shard_map/all_gather | solution.py:252
  366.0 623.8 %while.75 = (s32[]{:T(128)}, f32[192,256]{1,0:T(8,128)S(1)}, s32[32,49]{1,0:T(8,128)S(1)}, s32[]{:T(128)}, s32[]{:T(128)}, /*index=5*/bf16[32,1024,128]{2,1,0:T(...) while((s32[]{:T(128)}, f32[192,256]{1,0:T(8,128)S(1)}, ...), condition=%wide.region_25.27_spmd, body=%wide.region_22.26_spmd.sunk | while | flops 203110688 | bytes 4933767 | solution.py:276
  373.2 34.2 %conditional.11 = (f32[192,256]{1,0:T(8,128)S(1)}) conditional(s32[]{:T(128)} %convert_element_type.337, f32[192,256]{1,0:T(8,128)S(1)} %get-tuple-element.2741, (s32[3072]{0:T(1024)S(1)}, s32[]{:T(128)}, bf16[32,1024,128]{2,1,0:T(8,128)(2,1)}, s32[]{:T(128)}, bf16[192,128]{1,0:T(8,128)(2,1)S(1)}, /*index=5*/f32[32,1024]{1,0:T(8,128)S(1)}, ...), branch_computations={%region_23.24_spmd, %region_24.25_spmd.clone} | conditional | flops 203095296 | bytes 4882200 | solution.py:274
  409.8 34.2 %conditional.11 = (f32[192,256]{1,0:T(8,128)S(1)}) conditional(s32[]{:T(128)} %convert_element_type.337, f32[192,256]{1,0:T(8,128)S(1)} %get-tuple-element.2741, (s32[3072]{0:T(1024)S(1)}, s32[]{:T(128)}, bf16[32,1024,128]{2,1,0:T(8,128)(2,1)}, s32[]{:T(128)}, bf16[192,128]{1,0:T(8,128)(2,1)S(1)}, /*index=5*/f32[32,1024]{1,0:T(8,128)S(1)}, ...), branch_computations={%region_23.24_spmd, %region_24.25_spmd.clone} | conditional | flops 203095296 | bytes 4882200 | solution.py:274
  446.4 34.2 %conditional.11 = (f32[192,256]{1,0:T(8,128)S(1)}) conditional(s32[]{:T(128)} %convert_element_type.337, f32[192,256]{1,0:T(8,128)S(1)} %get-tuple-element.2741, (s32[3072]{0:T(1024)S(1)}, s32[]{:T(128)}, bf16[32,1024,128]{2,1,0:T(8,128)(2,1)}, s32[]{:T(128)}, bf16[192,128]{1,0:T(8,128)(2,1)S(1)}, /*index=5*/f32[32,1024]{1,0:T(8,128)S(1)}, ...), branch_computations={%region_23.24_spmd, %region_24.25_spmd.clone} | conditional | flops 203095296 | bytes 4882200 | solution.py:274
  490.2 34.2 %conditional.11 = (f32[192,256]{1,0:T(8,128)S(1)}) conditional(s32[]{:T(128)} %convert_element_type.337, f32[192,256]{1,0:T(8,128)S(1)} %get-tuple-element.2741, (s32[3072]{0:T(1024)S(1)}, s32[]{:T(128)}, bf16[32,1024,128]{2,1,0:T(8,128)(2,1)}, s32[]{:T(128)}, bf16[192,128]{1,0:T(8,128)(2,1)S(1)}, /*index=5*/f32[32,1024]{1,0:T(8,128)S(1)}, ...), branch_computations={%region_23.24_spmd, %region_24.25_spmd.clone} | conditional | flops 203095296 | bytes 4882200 | solution.py:274
  529.2 34.2 %conditional.11 = (f32[192,256]{1,0:T(8,128)S(1)}) conditional(s32[]{:T(128)} %convert_element_type.337, f32[192,256]{1,0:T(8,128)S(1)} %get-tuple-element.2741, (s32[3072]{0:T(1024)S(1)}, s32[]{:T(128)}, bf16[32,1024,128]{2,1,0:T(8,128)(2,1)}, s32[]{:T(128)}, bf16[192,128]{1,0:T(8,128)(2,1)S(1)}, /*index=5*/f32[32,1024]{1,0:T(8,128)S(1)}, ...), branch_computations={%region_23.24_spmd, %region_24.25_spmd.clone} | conditional | flops 203095296 | bytes 4882200 | solution.py:274
  570.6 34.2 %conditional.11 = (f32[192,256]{1,0:T(8,128)S(1)}) conditional(s32[]{:T(128)} %convert_element_type.337, f32[192,256]{1,0:T(8,128)S(1)} %get-tuple-element.2741, (s32[3072]{0:T(1024)S(1)}, s32[]{:T(128)}, bf16[32,1024,128]{2,1,0:T(8,128)(2,1)}, s32[]{:T(128)}, bf16[192,128]{1,0:T(8,128)(2,1)S(1)}, /*index=5*/f32[32,1024]{1,0:T(8,128)S(1)}, ...), branch_computations={%region_23.24_spmd, %region_24.25_spmd.clone} | conditional | flops 203095296 | bytes 4882200 | solution.py:274
  607.2 34.2 %conditional.11 = (f32[192,256]{1,0:T(8,128)S(1)}) conditional(s32[]{:T(128)} %convert_element_type.337, f32[192,256]{1,0:T(8,128)S(1)} %get-tuple-element.2741, (s32[3072]{0:T(1024)S(1)}, s32[]{:T(128)}, bf16[32,1024,128]{2,1,0:T(8,128)(2,1)}, s32[]{:T(128)}, bf16[192,128]{1,0:T(8,128)(2,1)S(1)}, /*index=5*/f32[32,1024]{1,0:T(8,128)S(1)}, ...), branch_computations={%region_23.24_spmd, %region_24.25_spmd.clone} | conditional | flops 203095296 | bytes 4882200 | solution.py:274
  643.7 34.2 %conditional.11 = (f32[192,256]{1,0:T(8,128)S(1)}) conditional(s32[]{:T(128)} %convert_element_type.337, f32[192,256]{1,0:T(8,128)S(1)} %get-tuple-element.2741, (s32[3072]{0:T(1024)S(1)}, s32[]{:T(128)}, bf16[32,1024,128]{2,1,0:T(8,128)(2,1)}, s32[]{:T(128)}, bf16[192,128]{1,0:T(8,128)(2,1)S(1)}, /*index=5*/f32[32,1024]{1,0:T(8,128)S(1)}, ...), branch_computations={%region_23.24_spmd, %region_24.25_spmd.clone} | conditional | flops 203095296 | bytes 4882200 | solution.py:274
  680.3 34.2 %conditional.11 = (f32[192,256]{1,0:T(8,128)S(1)}) conditional(s32[]{:T(128)} %convert_element_type.337, f32[192,256]{1,0:T(8,128)S(1)} %get-tuple-element.2741, (s32[3072]{0:T(1024)S(1)}, s32[]{:T(128)}, bf16[32,1024,128]{2,1,0:T(8,128)(2,1)}, s32[]{:T(128)}, bf16[192,128]{1,0:T(8,128)(2,1)S(1)}, /*index=5*/f32[32,1024]{1,0:T(8,128)S(1)}, ...), branch_computations={%region_23.24_spmd, %region_24.25_spmd.clone} | conditional | flops 203095296 | bytes 4882200 | solution.py:274
  721.7 34.2 %conditional.11 = (f32[192,256]{1,0:T(8,128)S(1)}) conditional(s32[]{:T(128)} %convert_element_type.337, f32[192,256]{1,0:T(8,128)S(1)} %get-tuple-element.2741, (s32[3072]{0:T(1024)S(1)}, s32[]{:T(128)}, bf16[32,1024,128]{2,1,0:T(8,128)(2,1)}, s32[]{:T(128)}, bf16[192,128]{1,0:T(8,128)(2,1)S(1)}, /*index=5*/f32[32,1024]{1,0:T(8,128)S(1)}, ...), branch_computations={%region_23.24_spmd, %region_24.25_spmd.clone} | conditional | flops 203095296 | bytes 4882200 | solution.py:274
  760.7 34.2 %conditional.11 = (f32[192,256]{1,0:T(8,128)S(1)}) conditional(s32[]{:T(128)} %convert_element_type.337, f32[192,256]{1,0:T(8,128)S(1)} %get-tuple-element.2741, (s32[3072]{0:T(1024)S(1)}, s32[]{:T(128)}, bf16[32,1024,128]{2,1,0:T(8,128)(2,1)}, s32[]{:T(128)}, bf16[192,128]{1,0:T(8,128)(2,1)S(1)}, /*index=5*/f32[32,1024]{1,0:T(8,128)S(1)}, ...), branch_computations={%region_23.24_spmd, %region_24.25_spmd.clone} | conditional | flops 203095296 | bytes 4882200 | solution.py:274
  799.7 34.2 %conditional.11 = (f32[192,256]{1,0:T(8,128)S(1)}) conditional(s32[]{:T(128)} %convert_element_type.337, f32[192,256]{1,0:T(8,128)S(1)} %get-tuple-element.2741, (s32[3072]{0:T(1024)S(1)}, s32[]{:T(128)}, bf16[32,1024,128]{2,1,0:T(8,128)(2,1)}, s32[]{:T(128)}, bf16[192,128]{1,0:T(8,128)(2,1)S(1)}, /*index=5*/f32[32,1024]{1,0:T(8,128)S(1)}, ...), branch_computations={%region_23.24_spmd, %region_24.25_spmd.clone} | conditional | flops 203095296 | bytes 4882200 | solution.py:274
  836.3 34.2 %conditional.11 = (f32[192,256]{1,0:T(8,128)S(1)}) conditional(s32[]{:T(128)} %convert_element_type.337, f32[192,256]{1,0:T(8,128)S(1)} %get-tuple-element.2741, (s32[3072]{0:T(1024)S(1)}, s32[]{:T(128)}, bf16[32,1024,128]{2,1,0:T(8,128)(2,1)}, s32[]{:T(128)}, bf16[192,128]{1,0:T(8,128)(2,1)S(1)}, /*index=5*/f32[32,1024]{1,0:T(8,128)S(1)}, ...), branch_computations={%region_23.24_spmd, %region_24.25_spmd.clone} | conditional | flops 203095296 | bytes 4882200 | solution.py:274
  875.3 34.2 %conditional.11 = (f32[192,256]{1,0:T(8,128)S(1)}) conditional(s32[]{:T(128)} %convert_element_type.337, f32[192,256]{1,0:T(8,128)S(1)} %get-tuple-element.2741, (s32[3072]{0:T(1024)S(1)}, s32[]{:T(128)}, bf16[32,1024,128]{2,1,0:T(8,128)(2,1)}, s32[]{:T(128)}, bf16[192,128]{1,0:T(8,128)(2,1)S(1)}, /*index=5*/f32[32,1024]{1,0:T(8,128)S(1)}, ...), branch_computations={%region_23.24_spmd, %region_24.25_spmd.clone} | conditional | flops 203095296 | bytes 4882200 | solution.py:274
  919.1 34.2 %conditional.11 = (f32[192,256]{1,0:T(8,128)S(1)}) conditional(s32[]{:T(128)} %convert_element_type.337, f32[192,256]{1,0:T(8,128)S(1)} %get-tuple-element.2741, (s32[3072]{0:T(1024)S(1)}, s32[]{:T(128)}, bf16[32,1024,128]{2,1,0:T(8,128)(2,1)}, s32[]{:T(128)}, bf16[192,128]{1,0:T(8,128)(2,1)S(1)}, /*index=5*/f32[32,1024]{1,0:T(8,128)S(1)}, ...), branch_computations={%region_23.24_spmd, %region_24.25_spmd.clone} | conditional | flops 203095296 | bytes 4882200 | solution.py:274
  955.7 34.2 %conditional.11 = (f32[192,256]{1,0:T(8,128)S(1)}) conditional(s32[]{:T(128)} %convert_element_type.337, f32[192,256]{1,0:T(8,128)S(1)} %get-tuple-element.2741, (s32[3072]{0:T(1024)S(1)}, s32[]{:T(128)}, bf16[32,1024,128]{2,1,0:T(8,128)(2,1)}, s32[]{:T(128)}, bf16[192,128]{1,0:T(8,128)(2,1)S(1)}, /*index=5*/f32[32,1024]{1,0:T(8,128)S(1)}, ...), branch_computations={%region_23.24_spmd, %region_24.25_spmd.clone} | conditional | flops 203095296 | bytes 4882200 | solution.py:274
  991.4 73.8 %all-reduce.1 = (f32[128]{0:T(128)}, f32[128]{0:T(128)}) all-reduce(f32[128]{0:T(128)S(1)} %multiply_reduce_fusion, f32[128]{0:T(128)S(1)} %add.301), channel_id=1, replica_groups=mesh['dp'=2,'seq'=32,'head'=4] {'dp','seq','head'}, use_global_device_ids=true, to_apply=%region_28.30 | all-reduce | flops 256 | bytes 2048 | tf_op jit(solution)/shard_map/psum | solution.py:284
  (590 shorter events, 809.7 us)
Async XLA Ops:
  7.2 180.3 %copy-start = (bf16[1,1,128,128]{3,2,1,0:T(8,128)(2,1)S(1)}, bf16[1,1,128,128]{3,2,1,0:T(8,128)(2,1)}, u32[]{:S(2)}) copy-start(bf16[1,1,128,128]{3,2,1,0:T(8,128)(2,1)} %param.38) | copy-start | bytes 98308
  7.2 86.1 %all-gather.9.cloned.1.call-start = ((), (), s32[]{:S(2)}) async-start(), calls=%async_computation.1 | async-start | bytes 1622016 | tf_op jit(solution)/shard_map/all_gather | solution.py:171
  8.1 0.6 copy-start.12
  8.7 0.6 copy-start.10
  10.8 157.9 %all-gather.15.cloned.1.call-start = ((), (), s32[]{:S(2)}) async-start(), calls=%async_computation.4 | async-start | bytes 1622016 | tf_op jit(solution)/shard_map/all_gather | solution.py:193
  11.6 312.0 %all-gather.11.cloned.1.call-start = ((), (), s32[]{:S(2)}) async-start(), calls=%async_computation.2 | async-start | bytes 8650752 | tf_op jit(solution)/shard_map/all_gather | solution.py:251
  15.1 350.9 %all-gather.13.cloned.1.call-start = ((), (), s32[]{:S(2)}) async-start(), calls=%async_computation.3 | async-start | bytes 8650752 | tf_op jit(solution)/shard_map/all_gather | solution.py:252
  24.8 162.7 %copy-start.2 = (bf16[1024,128]{0,1:T(8,128)(2,1)}, bf16[1024,128]{0,1:T(8,128)(2,1)S(1)}, u32[]{:S(2)}) copy-start(bf16[1024,128]{0,1:T(8,128)(2,1)S(1)} %select_convert_fusion.2) | copy-start | bytes 786436
  59.6 33.7 %copy-start.16 = (f32[128]{0:T(128)}, f32[128]{0:T(128)S(1)}, u32[]{:S(2)}) copy-start(f32[128]{0:T(128)S(1)} %fusion.125) | copy-start | bytes 1540
  93.2 94.6 %copy-start.3 = (f32[1024,128]{0,1:T(8,128)}, f32[1024,128]{0,1:T(8,128)S(1)}, u32[]{:S(2)}) copy-start(f32[1024,128]{0,1:T(8,128)S(1)} %get-tuple-element.2224) | copy-start | bytes 1572868
  168.8 20.1 %copy-start.7 = (bf16[1,1,128,128]{3,2,1,0:T(8,128)(2,1)S(1)}, bf16[1,1,128,128]{3,2,1,0:T(8,128)(2,1)}, u32[]{:S(2)}) copy-start(bf16[1,1,128,128]{3,2,1,0:T(8,128)(2,1)} %param.37) | copy-start | bytes 98308
  168.8 20.1 %copy-start.14 = (f32[128]{0:T(128)S(1)}, f32[128]{0:T(128)}, u32[]{:S(2)}) copy-start(f32[128]{0:T(128)} %param.40) | copy-start | bytes 1540
  188.1 0.7 copy-start.5
  189.4 31.8 %copy-start.15 = (f32[128]{0:T(128)S(1)}, f32[128]{0:T(128)}, u32[]{:S(2)}) copy-start(f32[128]{0:T(128)} %param.39) | copy-start | bytes 1540
  200.0 9.8 copy-start.1
  221.2 144.8 %copy-start.4 = (bf16[1,192,128]{2,1,0:T(8,128)(2,1)S(1)}, bf16[1,192,128]{2,1,0:T(8,128)(2,1)}, u32[]{:S(2)}) copy-start(bf16[1,192,128]{2,1,0:T(8,128)(2,1)} %param.35) | copy-start | bytes 147460
  221.2 144.8 %copy-start.8 = (s32[24,128]{1,0:T(8,128)S(1)}, s32[24,128]{1,0:T(8,128)}, u32[]{:S(2)}) copy-start(s32[24,128]{1,0:T(8,128)} %constant.495.clone.1) | copy-start | bytes 36868
  221.2 144.8 %copy-start.9 = (bf16[192,128]{1,0:T(8,128)(2,1)S(1)}, bf16[192,128]{1,0:T(8,128)(2,1)}, u32[]{:S(2)}) copy-start(bf16[192,128]{1,0:T(8,128)(2,1)} %fusion.112) | copy-start | bytes 147460
  227.3 93.9 %all-to-all-start = ((bf16[4,2,16384]{2,1,0:T(2,128)(2,1)}), bf16[4,2,16384]{2,1,0:T(2,128)(2,1)S(1)}, u32[]{:S(2)}, u32[]{:S(2)}) async-start(bf16[4,2,16384]{2,1,0:T(2,128)(2,1)} %reshape.734), calls=%async_computation | async-start | bytes 524288 | tf_op jit(solution)/shard_map/all_to_all | solution.py:285
  366.0 623.9 %copy-start.6 = (bf16[1,192,128]{2,1,0:T(8,128)(2,1)S(1)}, bf16[1,192,128]{2,1,0:T(8,128)(2,1)}, u32[]{:S(2)}) copy-start(bf16[1,192,128]{2,1,0:T(8,128)(2,1)} %param.34) | copy-start | bytes 147460
  366.0 623.9 %copy-start.11 = (f32[192]{0:T(256)S(1)}, f32[192]{0:T(256)}, u32[]{:S(2)}) copy-start(f32[192]{0:T(256)} %copy-done.10) | copy-start | bytes 2308
  366.0 624.6 %copy-start.13 = (f32[192]{0:T(256)S(1)}, f32[192]{0:T(256)}, u32[]{:S(2)}) copy-start(f32[192]{0:T(256)} %copy-done.12) | copy-start | bytes 2308
Sparse Core Ops, SparseCore 0:
  11.2 80.2 all-gather.8
  94.0 74.6 all-gather.14
  171.3 96.7 all-gather.10
  270.5 95.3 all-gather.12
where the time goes:
time: 1080 us; the launch traced here: 1070 us
  other arithmetic  544 us (50%)
  blocking collectives  181 us (17%)
  waiting for transfers between devices  100 us (9%)
  matrix products  96.7 us (9%)
  local copies, waits for them, and re-layouts  95 us (9%)
  loops' own time  33.2 us (3%)
  between operations  17 us (2%)
    gather x32, other arithmetic, repeat_mask(): jnp.repeat(tile_row, tile_size, total_repeat_length=tile_row.shape[0] * t...  444 us
    psum x1, blocking collectives, shards(): lax.psum((gain_query, prompt_gain_factor + response_gain_factor), ('dp',...  73.8 us
    gather x99, local copies, waits for them, and re-layouts, repeat_mask(): jnp.repeat(tile_row, tile_size, total_repeat_length=tile_row.shape[0] * t...  73.6 us
    gt x17, other arithmetic, repeat_mask(): jnp.repeat(tile_row, tile_size, total_repeat_length=tile_row.shape[0] * t...  69.4 us
    all_gather x1, waiting for transfers between devices, shards(): lax.all_gather(prompt_value_rows, 'seq', axis=0, tiled=True)  56.8 us
    all_gather x1, waiting for transfers between devices, shards(): lax.all_gather(grad_out[None], 'seq', axis=0, tiled=True)  42.4 us
    all_gather x1, blocking collectives, shards(): lax.all_gather(log_total[None], 'seq', axis=0, tiled=True)  41.9 us
    all_gather x1, blocking collectives, shards(): lax.all_gather(out_dot[None], 'seq', axis=0, tiled=True)  41.7 us
  transfers between devices with their start and end apart: 5, of which 2 were waited for; matrix products, arithmetic and copies ran while one was open for 10% of the time, Pallas kernels for 0%

commit v1 on v0

v1 whole, which is shorter than its diff:
```python
import functools

import jax
import jax.numpy as jnp
from jax import lax
from jax.experimental import pallas as pl
from jax.experimental.pallas import tpu as pltpu
from jax.sharding import Mesh
from jax.sharding import PartitionSpec as P

TILE = 64
HEAD = 128
HEADS = 8
TOKENS = 128
QUERIES = HEADS * TOKENS
ROWS = 192
Z = 8
Y = 4
X = 4
QUARTER = ROWS * Z // 2
CHUNK = 256
BLOCK = 256
PER_ROWS = ROWS // TILE
PER_PROMPT = PER_ROWS * Y
EPSILON = 1e-06
NEGATIVE = -1e30
SCALE = HEAD ** (-0.5)
SCALE2 = SCALE * 1.4426950408889634
VMEM = 56 * 1024 * 1024
F32 = jnp.float32
BF16 = jnp.bfloat16


def dot_nt(a, b):
    return lax.dot_general(a, b, (((1,), (1,)), ((), ())), preferred_element_type=F32)


def dot_nn(a, b):
    return jnp.dot(a, b, preferred_element_type=F32)


def dot_tn(a, b):
    return lax.dot_general(a, b, (((0,), (0,)), ((), ())), preferred_element_type=F32)


def unit(x):
    return x * lax.rsqrt(jnp.mean(x * x, axis=-1, keepdims=True) + EPSILON)


def norm_back(x, g, dy):
    r = lax.rsqrt(jnp.mean(x * x, axis=-1, keepdims=True) + EPSILON)
    u = x * r
    gy = g * dy
    return r * (gy - u * jnp.mean(u * gy, axis=-1, keepdims=True))


def responder(y, k):
    return lax.rem(y + (0, 1, 3, 2)[k], Y)


def responder_of(y, k):
    return lax.rem(y + jnp.where(k == 0, 0, jnp.where(k == 1, 1, jnp.where(k == 2, 3, 2))), Y)


def tile_bias(info, who, y, t):
    index = 1 + (t // PER_ROWS) * PER_PROMPT + y * PER_ROWS + t % PER_ROWS
    return jnp.where(info[who, index] > 0, 0.0, NEGATIVE).astype(F32)


def causal():
    v = lax.broadcasted_iota(jnp.int32, (TOKENS, TOKENS), 0)
    t = lax.broadcasted_iota(jnp.int32, (TOKENS, TOKENS), 1)
    return v <= t


def stats_kernel(pos, info, qg, kg, *refs):
    q = refs[:4]
    kv = refs[4:12]
    kr = refs[12]
    qh, kh, vh, ku, krh, out = refs[13:]
    y, z = pos[0], pos[1]
    for k in range(4):
        for j in range(HEADS):
            x = q[k][:, j * HEAD : (j + 1) * HEAD].astype(F32)
            qh[k, j * TOKENS : (j + 1) * TOKENS, :] = (unit(x) * qg[...]).astype(BF16)
    for s in range(Z):
        source = lax.rem(z + Z - (0, 1, 2, 3, 4, -1, -2, -3)[s], Z)
        rows = pl.ds(pl.multiple_of(source * ROWS, ROWS), ROWS)
        u = unit(kv[s][:, :HEAD].astype(F32))
        ku[rows, :] = u
        kh[rows, :] = (u * kg[...]).astype(BF16)
        vh[rows, :] = kv[s][:, HEAD:]
    krh[...] = (unit(kr[...].astype(F32)) * kg[...]).astype(BF16)
    mask = causal()

    def block(i, carry):
        k = i // 4
        b = i % 4
        who = responder_of(y, k)
        first = info[who, 0] * QUARTER
        qb = qh[k, pl.ds(pl.multiple_of(b * BLOCK, BLOCK), BLOCK), :]
        maxes, sums = [], []
        for c in range(QUARTER // CHUNK):
            keys = kh[pl.ds(pl.multiple_of(first + c * CHUNK, CHUNK), CHUNK), :]
            s = dot_nt(keys, qb) * SCALE2
            tiles = [s[t * TILE : (t + 1) * TILE] for t in range(CHUNK // TILE)]
            bias = [tile_bias(info, who, y, c * (CHUNK // TILE) + t) for t in range(CHUNK // TILE)]
            top = functools.reduce(
                jnp.maximum,
                [jnp.max(a, axis=0, keepdims=True) + v for a, v in zip(tiles, bias)],
            )
            top = jnp.maximum(top, 0.1 * NEGATIVE)
            sums.append(
                sum(
                    jnp.sum(jnp.exp2(a - (top - v)), axis=0, keepdims=True)
                    for a, v in zip(tiles, bias)
                )
            )
            maxes.append(top)
        top = functools.reduce(jnp.maximum, maxes)
        total = sum(s * jnp.exp2(m - top) for m, s in zip(maxes, sums))
        for h in range(BLOCK // TOKENS):
            for copy in range(Y):
                out[copy, who, pl.ds(b * 2 + h, 1), :] = top[:, h * TOKENS : (h + 1) * TOKENS]
                out[copy, who, pl.ds(8 + b * 2 + h, 1), :] = total[:, h * TOKENS : (h + 1) * TOKENS]
        return carry

    lax.fori_loop(0, 16, block, 0)
    for j in range(HEADS):
        s = dot_nt(krh[...], qh[0, j * TOKENS : (j + 1) * TOKENS, :]) * SCALE2
        s = jnp.where(mask, s, NEGATIVE)
        own = jnp.max(s, axis=0, keepdims=True)
        before = out[0, y, j : j + 1, :]
        top = jnp.maximum(own, before)
        total = jnp.sum(jnp.exp2(s - top), axis=0, keepdims=True)
        total = total + out[0, y, 8 + j : 9 + j, :] * jnp.exp2(before - top)
        for copy in range(Y):
            out[copy, y, j : j + 1, :] = top
            out[copy, y, 8 + j : 9 + j, :] = total


def values_kernel(pos, info, st, qh, kh, vh, krh, vr, *refs):
    go = refs[:4]
    dv, dvr, lt, out, gh = refs[4:]
    y = pos[0]
    for k in range(4):
        for j in range(HEADS):
            gh[k, j * TOKENS : (j + 1) * TOKENS, :] = go[k][:, j * HEAD : (j + 1) * HEAD]
        who = responder(y, k)
        top = functools.reduce(jnp.maximum, [st[s, who, 0:8, :] for s in range(Y)])
        total = sum(st[s, who, 8:16, :] * jnp.exp2(st[s, who, 0:8, :] - top) for s in range(Y))
        lt[k, :, :] = top + jnp.log2(total)
    dv[...] = jnp.zeros_like(dv)

    def block(i, carry):
        k = i // 4
        b = i % 4
        who = responder_of(y, k)
        first = info[who, 0] * QUARTER
        span = pl.ds(pl.multiple_of(b * BLOCK, BLOCK), BLOCK)
        qb = qh[k, span, :]
        gb = gh[k, span, :]
        row = jnp.concatenate([lt[k, pl.ds(b * 2 + h, 1), :] for h in range(2)], axis=1)
        dots = jnp.zeros((1, BLOCK), F32)
        for c in range(QUARTER // CHUNK):
            rows = pl.ds(pl.multiple_of(first + c * CHUNK, CHUNK), CHUNK)
            s = dot_nt(kh[rows, :], qb) * SCALE2
            g = dot_nt(vh[rows, :], gb)
            parts = []
            for t in range(CHUNK // TILE):
                v = tile_bias(info, who, y, c * (CHUNK // TILE) + t)
                span_t = slice(t * TILE, (t + 1) * TILE)
                p = jnp.exp2(s[span_t] - (row - v)).astype(BF16)
                parts.append(p)
                dots = dots + jnp.sum(p.astype(F32) * g[span_t], axis=0, keepdims=True)
            dv[rows, :] += dot_nn(jnp.concatenate(parts, axis=0), gb)
        for h in range(BLOCK // TOKENS):
            for copy in range(Y):
                out[copy, who, pl.ds(b * 2 + h, 1), :] = dots[:, h * TOKENS : (h + 1) * TOKENS]
        return carry

    lax.fori_loop(0, 16, block, 0)
    mask = causal()
    own = jnp.zeros((TOKENS, HEAD), F32)
    for j in range(HEADS):
        span = slice(j * TOKENS, (j + 1) * TOKENS)
        s = dot_nt(krh[...], qh[0, span, :]) * SCALE2
        p = jnp.where(mask, jnp.exp2(s - lt[0, j : j + 1, :]), 0.0).astype(BF16)
        g = dot_nt(vr[...], gh[0, span, :])
        dots = out[0, y, j : j + 1, :] + jnp.sum(p.astype(F32) * g, axis=0, keepdims=True)
        for copy in range(Y):
            out[copy, y, j : j + 1, :] = dots
        own = own + dot_nn(p, gh[0, span, :])
    dvr[...] = own


def grads_kernel(pos, info, dd, lt, qh, kh, vh, ku, krh, vr, gh, dv, qg, kg, kr, *refs):
    q = refs[:4]
    dq = refs[4:8]
    dkv, dkr, gains, kt, dots = refs[8:]
    y = pos[0]
    for k in range(4):
        who = responder(y, k)
        dots[k, :, :] = sum(dd[s, who, :, :] for s in range(Y))
    for p in range(2):
        kt[p, :, :] = kh[p * QUARTER : (p + 1) * QUARTER, :].T
    dkv[:, :HEAD] = jnp.zeros((2 * QUARTER, HEAD), F32)
    dkv[:, HEAD:] = dv[...]
    gains[...] = jnp.zeros_like(gains)

    def block_of(k, b):
        who = responder(y, k)
        group = info[who, 0]
        first = group * QUARTER
        span = pl.ds(pl.multiple_of(b * BLOCK, BLOCK), BLOCK)
        qb = qh[k, span, :]
        gb = gh[k, span, :]
        row = jnp.concatenate([lt[k, pl.ds(b * 2 + h, 1), :] for h in range(2)], axis=1)
        dot_row = jnp.concatenate([dots[k, pl.ds(b * 2 + h, 1), :] for h in range(2)], axis=1)
        total = jnp.zeros((HEAD, BLOCK), F32)
        for c in range(QUARTER // CHUNK):
            rows = pl.ds(pl.multiple_of(first + c * CHUNK, CHUNK), CHUNK)
            s = dot_nt(kh[rows, :], qb) * SCALE2
            g = dot_nt(vh[rows, :], gb)
            parts = []
            for t in range(CHUNK // TILE):
                v = tile_bias(info, who, y, c * (CHUNK // TILE) + t)
                span_t = slice(t * TILE, (t + 1) * TILE)
                p = jnp.exp2(s[span_t] - (row - v))
                parts.append((p * (g[span_t] - dot_row)).astype(BF16))
            ds = jnp.concatenate(parts, axis=0)
            dkv[rows, :HEAD] += dot_nn(ds, qb)
            total = total + dot_nn(kt[group, :, c * CHUNK : (c + 1) * CHUNK], ds)
        total = total * SCALE
        for h in range(BLOCK // TOKENS):
            lanes = pl.ds(pl.multiple_of(b * BLOCK + h * HEAD, HEAD), HEAD)
            dq[k][:, lanes] = total[:, h * TOKENS : (h + 1) * TOKENS].T

    mask = causal()
    for k in (3, 1, 2, 0):
        lax.fori_loop(0, 4, lambda b, carry, k=k: (block_of(k, b), carry)[1], 0)
    own = jnp.zeros((TOKENS, HEAD), F32)
    for j in range(HEADS):
        span = slice(j * TOKENS, (j + 1) * TOKENS)
        qb = qh[0, span, :]
        s = dot_nt(krh[...], qb) * SCALE2
        p = jnp.where(mask, jnp.exp2(s - lt[0, j : j + 1, :]), 0.0)
        g = dot_nt(vr[...], gh[0, span, :])
        ds = (p * (g - dots[0, j : j + 1, :])).astype(BF16)
        own = own + dot_nn(ds, qb)
        dq[0][:, j * HEAD : (j + 1) * HEAD] += dot_tn(ds, krh[...]) * SCALE
    dkv[:, :HEAD] = dkv[:, :HEAD] * SCALE
    own = own * SCALE
    x = kr[...].astype(F32)
    dkr[...] = norm_back(x, kg[...], own)
    gain_k = jnp.sum(dkv[:, :HEAD] * ku[...], axis=0, keepdims=True)
    gain_k = gain_k + jnp.sum(own * unit(x), axis=0, keepdims=True)
    gain_q = jnp.zeros((1, HEAD), F32)
    for k in range(4):
        for j in range(HEADS):
            span = slice(j * HEAD, (j + 1) * HEAD)
            gain_q = gain_q + jnp.sum(
                dq[k][:, span] * unit(q[k][:, span].astype(F32)), axis=0, keepdims=True
            )
    gains[0:1, :] = gain_q
    gains[1:2, :] = gain_k


def query_back_kernel(q, qg, mine, left, right, out):
    for j in range(HEADS):
        span = slice(j * HEAD, (j + 1) * HEAD)
        dy = mine[:, span] + left[:, span] + right[:, span]
        out[:, span] = norm_back(q[:, span].astype(F32), qg[...], dy).astype(BF16)


def key_back_kernel(k, kg, mine, left, right, dk, dv):
    dy = mine[...] + left[...] + right[...]
    dk[...] = norm_back(k[...].astype(F32), kg[...], dy[:, :HEAD])
    dv[...] = dy[:, HEAD:]


def spread_kernel(parts, out):
    for h in range(X):
        out[:, h * QUERIES : (h + 1) * QUERIES] = parts[h].astype(F32)


def call(kernel, out_shape, n_scalar, args, scratch=(), flops=0, nbytes=0):
    specs = [pl.BlockSpec(memory_space=pltpu.SMEM)] * n_scalar
    specs += [pl.BlockSpec(memory_space=pltpu.VMEM)] * (len(args) - n_scalar)
    return pl.pallas_call(
        kernel,
        out_shape=out_shape,
        in_specs=specs,
        out_specs=jax.tree.map(lambda _: pl.BlockSpec(memory_space=pltpu.VMEM), out_shape),
        scratch_shapes=scratch,
        compiler_params=pltpu.CompilerParams(vmem_limit_bytes=VMEM),
        cost_estimate=pl.CostEstimate(flops=flops, bytes_accessed=nbytes, transcendentals=0),
    )(*args)


def f32(*shape):
    return jax.ShapeDtypeStruct(shape, F32)


def bf16(*shape):
    return jax.ShapeDtypeStruct(shape, BF16)


def shift(x, axis, size, step):
    return lax.ppermute(x, axis, [(i, (i + step) % size) for i in range(size)])


def to_all(x, axis):
    return lax.all_to_all(x, axis, 0, 0, tiled=False)


def shards(
    prompt_key_input,
    prompt_value_input,
    resp_queries,
    response_key_input,
    response_value_input,
    q_gain,
    k_gain,
    groups,
    lengths,
    tiles,
    advantages,
    upstream,
):
    y = lax.axis_index("y")
    z = lax.axis_index("z")
    pos = jnp.stack([y, z]).astype(jnp.int32)
    qg = q_gain[None]
    kg = k_gain[None]
    k_raw = prompt_key_input[0]
    q_raw = resp_queries[0, 0]
    kr = response_key_input[0, 0]
    vr = response_value_input[0, 0]
    info = jnp.concatenate([groups[0], tiles[0, 0], jnp.zeros((79,), jnp.int32)])
    info = to_all(jnp.broadcast_to(info[None], (Y, 128)), "y").reshape(Y, 128)

    kv = jnp.concatenate([k_raw, prompt_value_input[0]], axis=1)
    q_before = shift(q_raw, "y", Y, 1)
    q_next = shift(q_raw, "y", Y, -1)
    q_far = shift(q_before, "y", Y, 1)
    up = [kv]
    down = []
    for s in range(Z // 2):
        up.append(shift(up[-1], "z", Z, 1))
        if s < Z // 2 - 1:
            down.append(shift(down[-1] if down else kv, "z", Z, -1))
    tokens = jnp.arange(TOKENS, dtype=jnp.int32)[:, None]
    go = jnp.where(
        tokens < lengths[0, 0], -advantages[0, 0] * upstream[0, 0].astype(F32), 0.0
    ).astype(BF16)
    go_before = shift(go, "y", Y, 1)
    go_next = shift(go, "y", Y, -1)
    go_far = shift(go_next, "y", Y, -1)
    qs = (q_raw, q_next, q_before, q_far)
    gos = (go, go_next, go_before, go_far)

    unit_flops = 2 * 4 * QUERIES * QUARTER * HEAD
    qh, kh, vh, ku, krh, st = call(
        stats_kernel,
        (
            bf16(4, QUERIES, HEAD),
            bf16(2 * QUARTER, HEAD),
            bf16(2 * QUARTER, HEAD),
            f32(2 * QUARTER, HEAD),
            bf16(TOKENS, HEAD),
            f32(Y, Y, 16, 128),
        ),
        2,
        (pos, info, qg, kg, *qs, *up, *down, kr),
        flops=2 * unit_flops,
        nbytes=1 << 22,
    )
    st = to_all(st, "y")
    dv, dvr, lt, dd, gh = call(
        values_kernel,
        (
            f32(2 * QUARTER, HEAD),
            f32(TOKENS, HEAD),
            f32(4, HEADS, 128),
            f32(Y, Y, HEADS, 128),
            bf16(4, QUERIES, HEAD),
        ),
        2,
        (pos, info, st, qh, kh, vh, krh, vr, *gos),
        flops=4 * unit_flops,
        nbytes=1 << 22,
    )
    dd = to_all(dd, "y")
    dq0, dq1, dq2, dq3, dkv, dkr, gains = call(
        grads_kernel,
        (
            *[f32(TOKENS, QUERIES)] * 4,
            f32(2 * QUARTER, 2 * HEAD),
            f32(TOKENS, HEAD),
            f32(8, HEAD),
        ),
        2,
        (pos, info, dd, lt, qh, kh, vh, ku, krh, vr, gh, dv, qg, kg, kr, *qs),
        scratch=[
            pltpu.VMEM((2, HEAD, QUARTER), BF16),
            pltpu.VMEM((4, HEADS, 128), F32),
        ],
        flops=5 * unit_flops,
        nbytes=1 << 22,
    )

    half = QUERIES // 2
    far_up = shift(dq3[:, :half], "y", Y, 1)
    far_down = shift(dq3[:, half:], "y", Y, -1)
    to_next = jnp.concatenate([dq1[:, :half] + far_up, dq1[:, half:]], axis=1)
    to_before = jnp.concatenate([dq2[:, :half], dq2[:, half:] + far_down], axis=1)
    from_before = shift(to_next, "y", Y, 1)
    from_next = shift(to_before, "y", Y, -1)

    dkv = dkv.reshape(Z, ROWS, 2 * HEAD)

    def piece(step):
        return lax.dynamic_index_in_dim(dkv, lax.rem(z + step + Z, Z), 0, keepdims=False)

    rising = shift(piece(4), "z", Z, 1)
    falling = shift(piece(-3), "z", Z, -1)
    for s in (3, 2, 1):
        rising = shift(rising + piece(s), "z", Z, 1)
        if s > 1:
            falling = shift(falling + piece(1 - s), "z", Z, -1)

    dq = call(
        query_back_kernel,
        bf16(TOKENS, QUERIES),
        0,
        (q_raw, qg, dq0, from_before, from_next),
        nbytes=1 << 21,
    )
    dq = to_all(dq.reshape(X, TOKENS // X, QUERIES), "head")
    regrouped = call(spread_kernel, f32(TOKENS // X, X * QUERIES), 0, (dq,), nbytes=1 << 20)
    dk, dv = call(
        key_back_kernel,
        (f32(ROWS, HEAD), f32(ROWS, HEAD)),
        0,
        (k_raw, kg, piece(0), rising, falling),
        nbytes=1 << 20,
    )
    gains = gains[:2]
    gains = gains + lax.ppermute(gains, "dp", [(0, 1), (1, 0)])
    for axis, size in (("head", X), ("y", Y), ("z", Z)):
        gains = jnp.sum(to_all(jnp.broadcast_to(gains[None], (size, 2, HEAD)), axis), axis=0)
    return (
        regrouped[None, None],
        dkr[None, None],
        dvr[None, None],
        dk[None],
        dv[None],
        gains[0],
        gains[1],
    )


def solution(mesh):
    sizes = mesh.devices.shape
    split = Mesh(mesh.devices.reshape(sizes[0], Z, Y, sizes[2]), ("dp", "z", "y", "head"))
    seq = ("z", "y")
    placed = (
        P("dp", seq, "head"),
        P("dp", seq, "head"),
        P("dp", seq, None, "head"),
        P("dp", seq, None, "head"),
        P("dp", seq, None, "head"),
        P(),
        P(),
        P("dp", seq),
        P("dp", seq),
        P("dp", seq, None),
        P("dp", seq),
        P("dp", seq, None, "head"),
    )
    return jax.shard_map(
        shards,
        mesh=split,
        in_specs=placed,
        out_specs=(
            P("dp", seq, "head", None),
            P("dp", seq, None, "head"),
            P("dp", seq, None, "head"),
            P("dp", seq, "head"),
            P("dp", seq, "head"),
            P(),
            P(),
        ),
        check_vma=False,
    )
```

time: 1080 us -> 180 us (0.17)
  other arithmetic: 544 us -> 7.65 us
  blocking collectives: 181 us -> 17.4 us
  matrix products: 96.7 us -> 0 us
  local copies, waits for them, and re-layouts: 95 us -> 9.32 us
  waiting for transfers between devices: 100 us -> 32.9 us
  starting transfers between devices: 4.94 us -> 56.6 us
  Pallas kernels: 0 us -> 51.4 us
  loops' own time: 33.2 us -> 0 us
  between operations: 17 us -> 2.99 us
    gather x32 -> x0, other arithmetic: 444 us -> none  [repeat_mask(): jnp.repeat(tile_row, tile_size, total_repeat_length=tile_row.shape[0] * t...]
    all_gather x4 -> x0, waiting for transfers between devices: 99.2 us -> none  [the longest x1 56.8 us: shards(): lax.all_gather(prompt_value_rows, 'seq', axis=0, tiled=True)]
    dot_general x58 -> x0, matrix products: 96.7 us -> none  [the longest x19 33 us: raw_scores(): jnp.dot(query_hat, key_block.T, preferred_element_type=jnp.float32)]
    all_gather x2 -> x0, blocking collectives: 83.6 us -> none  [the longest x1 41.9 us: shards(): lax.all_gather(log_total[None], 'seq', axis=0, tiled=True)]
    psum x1 -> x0, blocking collectives: 73.8 us -> none  [shards(): lax.psum((gain_query, prompt_gain_factor + response_gain_factor), ('dp',...]
    gather x99 -> x0, local copies, waits for them, and re-layouts: 73.6 us -> none  [repeat_mask(): jnp.repeat(tile_row, tile_size, total_repeat_length=tile_row.shape[0] * t...]
    gt x17 -> x0, other arithmetic: 69.4 us -> none  [repeat_mask(): jnp.repeat(tile_row, tile_size, total_repeat_length=tile_row.shape[0] * t...]
    pallas_call x0 -> x6, Pallas kernels: none -> 51.4 us  [call(): pl.pallas_call(kernel, out_shape=out_shape, in_specs=specs, out_specs=jax...]
  transfers between devices with their start and end apart: 5 -> 30, of which waited for: 2 -> 9; matrix products, arithmetic and copies ran while one was open for 10% -> 6% of each run, Pallas kernels for 0% -> 9%
where the time goes in v1:
time: 180 us; the launch traced here: 178 us
  starting transfers between devices  56.6 us (31%)
  Pallas kernels  51.4 us (29%)
  waiting for transfers between devices  32.9 us (18%)
  blocking collectives  17.4 us (10%)
  local copies, waits for them, and re-layouts  9.32 us (5%)
  other arithmetic  7.65 us (4%)
  between operations  2.99 us (2%)
    pallas_call x6, Pallas kernels, call(): pl.pallas_call(kernel, out_shape=out_shape, in_specs=specs, out_specs=jax...  51.4 us
    ppermute x24, starting transfers between devices, shift(): return lax.ppermute(x, axis, [(i, (i + step) % size) for i in range(size)])  35.3 us
    all_to_all x5, starting transfers between devices, to_all(): return lax.all_to_all(x, axis, 0, 0, tiled=False)  21.3 us
    all_to_all x5, waiting for transfers between devices, to_all(): return lax.all_to_all(x, axis, 0, 0, tiled=False)  20.6 us
    all_to_all x2, blocking collectives, to_all(): return lax.all_to_all(x, axis, 0, 0, tiled=False)  17.4 us
    ppermute x24, waiting for transfers between devices, shift(): return lax.ppermute(x, axis, [(i, (i + step) % size) for i in range(size)])  12.3 us
    unnamed x54, local copies, waits for them, and re-layouts  4.43 us
  transfers between devices with their start and end apart: 30, of which 9 were waited for; matrix products, arithmetic and copies ran while one was open for 6% of the time, Pallas kernels for 9%

profile of v1, /device:TPU:6, one launch (start us, length us, event | category | flops | bytes accessed | tf_op | source)
XLA Modules:
  0.0 178.2 jit_solution(14279264905481361593)
XLA Ops:
  4.8 2.0 %collective-permute-start.3 = (bf16[192,256]{1,0:T(8,128)(2,1)S(1)}, bf16[192,256]{1,0:T(8,128)(2,1)S(1)}, u32[]{:S(2)}, u32[]{:S(2)}) collective-permute-start(bf16[192,256]{1,0:T(8,128)(2,1)S(1)} %pad_maximum_fusion.2.refs_4_), channel_id=1, source_target_pairs={{0,16},{16,32},{32,48},{48,64},{64,80},{80,96},{96,112},{112,0},{1... | collective-permute-start | bytes 294920 | tf_op jit(solution)/shard_map/ppermute | solution.py:310
  11.1 3.9 %collective-permute-start.7 = (bf16[192,256]{1,0:T(8,128)(2,1)S(1)}, bf16[192,256]{1,0:T(8,128)(2,1)S(1)}, u32[]{:S(2)}, u32[]{:S(2)}) collective-permute-start(bf16[192,256]{1,0:T(8,128)(2,1)S(1)} %pad_maximum_fusion.2.refs_4_), channel_id=1, source_target_pairs={{0,112},{16,0},{32,16},{48,32},{64,48},{80,64},{96,80},{112,96},{1... | collective-permute-start | bytes 294920 | tf_op jit(solution)/shard_map/ppermute | solution.py:310
  17.2 3.6 %collective-permute-start.8 = (bf16[192,256]{1,0:T(8,128)(2,1)S(1)}, bf16[192,256]{1,0:T(8,128)(2,1)S(1)}, u32[]{:S(2)}, u32[]{:S(2)}) collective-permute-start(bf16[192,256]{1,0:T(8,128)(2,1)S(1)} %collective-permute-done.7.refs_9_), channel_id=1, source_target_pairs={{0,112},{16,0},{32,16},{48,32},{64,48},{80,64},{96,80},{112,96},{1... | collective-permute-start | bytes 294920 | tf_op jit(solution)/shard_map/ppermute | solution.py:310
  22.2 3.2 %all-to-all-start = ((s32[4,1,128]{2,1,0:T(1,128)}), s32[4,1,128]{2,1,0:T(1,128)S(1)}, u32[]{:S(2)}, u32[]{:S(2)}) async-start(s32[4,1,128]{2,1,0:T(1,128)} %broadcast_in_dim.63), calls=%async_computation | async-start | bytes 4096 | tf_op jit(solution)/shard_map/all_to_all | solution.py:314
  27.4 3.2 %collective-permute-start.9 = (bf16[192,256]{1,0:T(8,128)(2,1)S(1)}, bf16[192,256]{1,0:T(8,128)(2,1)S(1)}, u32[]{:S(2)}, u32[]{:S(2)}) collective-permute-start(bf16[192,256]{1,0:T(8,128)(2,1)S(1)} %collective-permute-done.8.refs_10_), channel_id=1, source_target_pairs={{0,112},{16,0},{32,16},{48,32},{64,48},{80,64},{96,80},{112,96},{1... | collective-permute-start | bytes 294920 | tf_op jit(solution)/shard_map/ppermute | solution.py:310
  32.8 5.0 %collective-permute-done.6.refs_8_ = bf16[192,256]{1,0:T(8,128)(2,1)S(1)} collective-permute-done((bf16[192,256]{1,0:T(8,128)(2,1)S(1)}, bf16[192,256]{1,0:T(8,128)(2,1)S(1)}, u32[]{:S(2)}, u32[]{:S(2)}) %collective-permute-start.6) | collective-permute-done | bytes 98336 | tf_op jit(solution)/shard_map/ppermute | solution.py:310
  38.6 10.4 %shard_map.171 = (bf16[4,1024,128]{2,1,0:T(8,128)(2,1)}, bf16[1536,128]{1,0:T(8,128)(2,1)}, bf16[1536,128]{1,0:T(8,128)(2,1)}, f32[1536,128]{1,0:T(8,128)}, bf16...) custom-call(s32[2]{0:T(128)} %pad_add_fusion.pos, s32[4,128]{1,0:T(4,128)} %bitcast.61, f32[1,128]{1,0:T(1,128)} %bitcast.64, ...), custom_call_target="tpu_custom_call" | custom-call | flops 1610612736 | bytes 4194304 | tf_op jit(solution)/shard_map/pallas_call | solution.py:290
  49.0 3.5 %all-to-all-start.1 = ((f32[4,4,16,128]{3,2,1,0:T(8,128)}), f32[4,4,16,128]{3,2,1,0:T(8,128)S(1)}, u32[]{:S(2)}, u32[]{:S(2)}) async-start(f32[4,4,16,128]{3,2,1,0:T(8,128)} %get-tuple-element.27), calls=%async_computation.1 | async-start | bytes 262144 | tf_op jit(solution)/shard_map/all_to_all | solution.py:314
  52.6 5.9 %all-to-all-done.1.st = f32[4,4,16,128]{3,2,1,0:T(8,128)S(1)} async-done(((f32[4,4,16,128]{3,2,1,0:T(8,128)}), f32[4,4,16,128]{3,2,1,0:T(8,128)S(1)}, u32[]{:S(2)}, u32[]{:S(2)}) %all-to-all-start.1) | async-done | bytes 131104 | tf_op jit(solution)/shard_map/all_to_all | solution.py:314
  59.1 13.8 %shard_map.172 = (f32[1536,128]{1,0:T(8,128)}, f32[128,128]{1,0:T(8,128)}, f32[4,8,128]{2,1,0:T(8,128)}, f32[4,4,8,128]{3,2,1,0:T(8,128)}, bf16[4,1024,128]{2,1,0:T(8,128)(2,1)}) custom-call(s32[2]{0:T(128)} %pad_add_fusion.pos, s32[4,128]{1,0:T(4,128)} %bitcast.62, f32[4,4,16,128]{3,2,1,0:T(8,128)} %copy-done.9, ...), custom_call_target="tpu_custom_call" | custom-call | flops 3221225472 | bytes 4194304 | tf_op jit(solution)/shard_map/pallas_call | solution.py:290
  72.9 3.3 %all-to-all-start.2 = ((f32[4,4,8,128]{3,2,1,0:T(8,128)}), f32[4,4,8,128]{3,2,1,0:T(8,128)S(1)}, u32[]{:S(2)}, u32[]{:S(2)}) async-start(f32[4,4,8,128]{3,2,1,0:T(8,128)} %get-tuple-element.32), calls=%async_computation.2 | async-start | bytes 131072 | tf_op jit(solution)/shard_map/all_to_all | solution.py:314
  76.2 5.6 %all-to-all-done.2.dd = f32[4,4,8,128]{3,2,1,0:T(8,128)S(1)} async-done(((f32[4,4,8,128]{3,2,1,0:T(8,128)}), f32[4,4,8,128]{3,2,1,0:T(8,128)S(1)}, u32[]{:S(2)}, u32[]{:S(2)}) %all-to-all-start.2) | async-done | bytes 65568 | tf_op jit(solution)/shard_map/all_to_all | solution.py:314
  82.4 20.6 %shard_map.173 = (f32[128,1024]{1,0:T(8,128)}, f32[128,1024]{1,0:T(8,128)}, f32[128,1024]{1,0:T(8,128)}, f32[128,1024]{1,0:T(8,128)}, f32[1536,256]{1,0:T(8,128)}, /*index=5*/f32[128,128]{1,0:T(8,128)}, f32[8,128]{1,0:T(8,128)}) custom-call(s32[2]{0:T(128)} %pad_add_fusion.pos, s32[4,128]{1,0:T(4,128)} %bitcast.63, f32[4,4,8,128]{3,2,1,0:T(8,128)} %copy-done.11, ...), custom_call_target="tpu_custom_call" | custom-call | flops 4026531840 | bytes 4194304 | tf_op jit(solution)/shard_map/pallas_call | solution.py:290
  103.1 2.1 %dynamic-slice_bitcast_fusion = (f32[192,256]{1,0:T(8,128)}, f32[192,256]{1,0:T(8,128)}, f32[192,256]{1,0:T(8,128)}) fusion(f32[8,192,256]{2,1,0:T(8,128)} %bitcast.47, s32[]{:T(128)S(6)} %select_n.35, s32[]{:T(128)S(6)} %select_n.31, s32[]{:T(128)S(6)} %select_n.30), kind=kLoop, calls=%fused_computation.11 | loop fusion | bytes 1179660 | tf_op jit(solution)/shard_map/jit(dynamic_index_in_dim)/squeeze | solution.py:424
  107.5 3.3 %collective-permute-start.21 = (f32[192,256]{1,0:T(8,128)}, f32[192,256]{1,0:T(8,128)S(1)}, u32[]{:S(2)}, u32[]{:S(2)}) collective-permute-start(f32[192,256]{1,0:T(8,128)} %get-tuple-element.51), channel_id=1, source_target_pairs={{0,112},{16,0},{32,16},{48,32},{64,48},{80,64},{96,80},{112,96},{1... | collective-permute-start | bytes 589832 | tf_op jit(solution)/shard_map/ppermute | solution.py:310
  115.3 5.1 %collective-permute-done.13 = f32[128,512]{1,0:T(8,128)S(1)} collective-permute-done((f32[128,512]{1,0:T(8,128)S(1)}, f32[128,512]{1,0:T(8,128)S(1)}, u32[]{:S(2)}, u32[]{:S(2)}) %collective-permute-start.13) | collective-permute-done | bytes 262176 | tf_op jit(solution)/shard_map/ppermute | solution.py:310
  122.1 3.2 %collective-permute-start.22 = (f32[192,256]{1,0:T(8,128)S(1)}, f32[192,256]{1,0:T(8,128)}, u32[]{:S(2)}, u32[]{:S(2)}) collective-permute-start(f32[192,256]{1,0:T(8,128)S(1)} %get-tuple-element.49), channel_id=1, source_target_pairs={{0,112},{16,0},{32,16},{48,32},{64,48},{80,64},{96,80},{112,96},{1... | collective-permute-start | bytes 589832 | tf_op jit(solution)/shard_map/ppermute | solution.py:310
  125.3 7.8 %all_to_all.38 = f32[4,2,128]{2,1,0:T(2,128)S(1)} all-to-all(f32[4,2,128]{2,1,0:T(2,128)S(1)} %broadcast_in_dim.72), channel_id=1, replica_groups=mesh['dp'=2,'z'=8,'y'=4,'head'=4] {'head'}, dimensions={0} | all-to-all | bytes 8192 | tf_op jit(solution)/shard_map/all_to_all | solution.py:314
  133.1 9.6 %all_to_all.39 = f32[4,2,128]{2,1,0:T(2,128)S(1)} all-to-all(f32[4,2,128]{2,1,0:T(2,128)S(1)} %broadcast_in_dim.73), channel_id=1, replica_groups=mesh['dp'=2,'z'=8,'y'=4,'head'=4] {'y'}, dimensions={0} | all-to-all | bytes 8192 | tf_op jit(solution)/shard_map/all_to_all | solution.py:314
  143.3 5.8 %all-to-all-start.6 = ((f32[8,2,128]{2,1,0:T(2,128)}), f32[8,2,128]{2,1,0:T(2,128)S(1)}, u32[]{:S(2)}, u32[]{:S(2)}) async-start(f32[8,2,128]{2,1,0:T(2,128)} %broadcast_in_dim.74), calls=%async_computation.6 | async-start | bytes 16384 | tf_op jit(solution)/shard_map/all_to_all | solution.py:314
  149.2 7.8 %all-to-all-done.6 = f32[8,2,128]{2,1,0:T(2,128)S(1)} async-done(((f32[8,2,128]{2,1,0:T(2,128)}), f32[8,2,128]{2,1,0:T(2,128)S(1)}, u32[]{:S(2)}, u32[]{:S(2)}) %all-to-all-start.6) | async-done | bytes 8224 | tf_op jit(solution)/shard_map/all_to_all | solution.py:314
  159.3 2.6 %collective-permute-start.23 = (f32[192,256]{1,0:T(8,128)S(1)}, f32[192,256]{1,0:T(8,128)S(1)}, u32[]{:S(2)}, u32[]{:S(2)}) collective-permute-start(f32[192,256]{1,0:T(8,128)S(1)} %get-tuple-element.47), channel_id=1, source_target_pairs={{0,112},{16,0},{32,16},{48,32},{64,48},{80,64},{96,80},{112,96},{1... | collective-permute-start | bytes 589832 | tf_op jit(solution)/shard_map/ppermute | solution.py:310
  162.9 2.8 %shard_map.174 = bf16[128,1024]{1,0:T(8,128)(2,1)} custom-call(bf16[128,1024]{1,0:T(8,128)(2,1)} %bitcast.57, f32[1,128]{1,0:T(1,128)} %bitcast.66, f32[128,1024]{1,0:T(8,128)} %get-tuple-element.37.mine, f32[128,1024]{1,0:T(8,128)} %copy-done.3, f32[128,1024]{1,0:T(8,128)} %copy-done.2), custom_call_target="tpu_custom_call" | custom-call | bytes 2097152 | tf_op jit(solution)/shard_map/pallas_call | solution.py:290
  165.7 5.4 %all-to-all-start.3 = ((bf16[4,32,1024]{2,1,0:T(8,128)(2,1)}), bf16[4,32,1024]{2,1,0:T(8,128)(2,1)S(1)}, u32[]{:S(2)}, u32[]{:S(2)}) async-start(bf16[4,32,1024]{2,1,0:T(8,128)(2,1)} %bitcast.51), calls=%async_computation.3 | async-start | bytes 524288 | tf_op jit(solution)/shard_map/all_to_all | solution.py:314
  (123 shorter events, 35.6 us)
Async XLA Ops:
  0.6 14.4 %collective-permute-start.1 = (bf16[128,1024]{1,0:T(8,128)(2,1)}, bf16[128,1024]{1,0:T(8,128)(2,1)S(1)}, u32[]{:S(2)}, u32[]{:S(2)}) collective-permute-start(bf16[128,1024]{1,0:T(8,128)(2,1)} %bitcast.53), channel_id=1, source_target_pairs={{0,4},{4,8},{8,12},{12,0},{1,5},{5,9},{9,13},{13,1},{2,6},{6,10},{... | collective-permute-start | bytes 786440 | tf_op jit(solution)/shard_map/ppermute | solution.py:310
  2.3 25.1 %collective-permute-start = (bf16[128,1024]{1,0:T(8,128)(2,1)}, bf16[128,1024]{1,0:T(8,128)(2,1)S(1)}, u32[]{:S(2)}, u32[]{:S(2)}) collective-permute-start(bf16[128,1024]{1,0:T(8,128)(2,1)} %bitcast.54), channel_id=1, source_target_pairs={{0,12},{4,0},{8,4},{12,8},{1,13},{5,1},{9,5},{13,9},{2,14},{6,2},{... | collective-permute-start | bytes 786440 | tf_op jit(solution)/shard_map/ppermute | solution.py:310
  4.8 10.2 %collective-permute-start.3 = (bf16[192,256]{1,0:T(8,128)(2,1)S(1)}, bf16[192,256]{1,0:T(8,128)(2,1)S(1)}, u32[]{:S(2)}, u32[]{:S(2)}) collective-permute-start(bf16[192,256]{1,0:T(8,128)(2,1)S(1)} %pad_maximum_fusion.2.refs_4_), channel_id=1, source_target_pairs={{0,16},{16,32},{32,48},{48,64},{64,80},{80,96},{96,112},{112,0},{1... | collective-permute-start | bytes 294920 | tf_op jit(solution)/shard_map/ppermute | solution.py:310
  9.2 21.4 %collective-permute-start.10 = (bf16[128,1024]{1,0:T(8,128)(2,1)S(1)}, bf16[128,1024]{1,0:T(8,128)(2,1)S(1)}, u32[]{:S(2)}, u32[]{:S(2)}) collective-permute-start(bf16[128,1024]{1,0:T(8,128)(2,1)S(1)} %fusion.refs_0_), channel_id=1, source_target_pairs={{0,12},{4,0},{8,4},{12,8},{1,13},{5,1},{9,5},{13,9},{2,14},{6,2},{... | collective-permute-start | bytes 786440 | tf_op jit(solution)/shard_map/ppermute | solution.py:310
  15.0 22.8 %collective-permute-start.2 = (bf16[128,1024]{1,0:T(8,128)(2,1)S(1)}, bf16[128,1024]{1,0:T(8,128)(2,1)S(1)}, u32[]{:S(2)}, u32[]{:S(2)}) collective-permute-start(bf16[128,1024]{1,0:T(8,128)(2,1)S(1)} %collective-permute-done.1.refs_2_), channel_id=1, source_target_pairs={{0,4},{4,8},{8,12},{12,0},{1,5},{5,9},{9,13},{13,1},{2,6},{6,10},{... | collective-permute-start | bytes 786440 | tf_op jit(solution)/shard_map/ppermute | solution.py:310
  17.2 8.2 %collective-permute-start.8 = (bf16[192,256]{1,0:T(8,128)(2,1)S(1)}, bf16[192,256]{1,0:T(8,128)(2,1)S(1)}, u32[]{:S(2)}, u32[]{:S(2)}) collective-permute-start(bf16[192,256]{1,0:T(8,128)(2,1)S(1)} %collective-permute-done.7.refs_9_), channel_id=1, source_target_pairs={{0,112},{16,0},{32,16},{48,32},{64,48},{80,64},{96,80},{112,96},{1... | collective-permute-start | bytes 294920 | tf_op jit(solution)/shard_map/ppermute | solution.py:310
  20.8 11.1 %collective-permute-start.5 = (bf16[192,256]{1,0:T(8,128)(2,1)S(1)}, bf16[192,256]{1,0:T(8,128)(2,1)S(1)}, u32[]{:S(2)}, u32[]{:S(2)}) collective-permute-start(bf16[192,256]{1,0:T(8,128)(2,1)S(1)} %collective-permute-done.4.refs_6_), channel_id=1, source_target_pairs={{0,16},{16,32},{32,48},{48,64},{64,80},{80,96},{96,112},{112,0},{1... | collective-permute-start | bytes 294920 | tf_op jit(solution)/shard_map/ppermute | solution.py:310
  22.2 10.4 %all-to-all-start = ((s32[4,1,128]{2,1,0:T(1,128)}), s32[4,1,128]{2,1,0:T(1,128)S(1)}, u32[]{:S(2)}, u32[]{:S(2)}) async-start(s32[4,1,128]{2,1,0:T(1,128)} %broadcast_in_dim.63), calls=%async_computation | async-start | bytes 4096 | tf_op jit(solution)/shard_map/all_to_all | solution.py:314
  25.4 27.1 %collective-permute-start.11 = (bf16[128,1024]{1,0:T(8,128)(2,1)S(1)}, bf16[128,1024]{1,0:T(8,128)(2,1)S(1)}, u32[]{:S(2)}, u32[]{:S(2)}) collective-permute-start(bf16[128,1024]{1,0:T(8,128)(2,1)S(1)} %fusion.refs_0_), channel_id=1, source_target_pairs={{0,4},{4,8},{8,12},{12,0},{1,5},{5,9},{9,13},{13,1},{2,6},{6,10},{... | collective-permute-start | bytes 786440 | tf_op jit(solution)/shard_map/ppermute | solution.py:310
  30.6 21.9 %collective-permute-start.12 = (bf16[128,1024]{1,0:T(8,128)(2,1)S(1)}, bf16[128,1024]{1,0:T(8,128)(2,1)S(1)}, u32[]{:S(2)}, u32[]{:S(2)}) collective-permute-start(bf16[128,1024]{1,0:T(8,128)(2,1)S(1)} %collective-permute-done.10.refs_1_), channel_id=1, source_target_pairs={{0,12},{4,0},{8,4},{12,8},{1,13},{5,1},{9,5},{13,9},{2,14},{6,2},{... | collective-permute-start | bytes 786440 | tf_op jit(solution)/shard_map/ppermute | solution.py:310
  49.0 9.4 %all-to-all-start.1 = ((f32[4,4,16,128]{3,2,1,0:T(8,128)}), f32[4,4,16,128]{3,2,1,0:T(8,128)S(1)}, u32[]{:S(2)}, u32[]{:S(2)}) async-start(f32[4,4,16,128]{3,2,1,0:T(8,128)} %get-tuple-element.27), calls=%async_computation.1 | async-start | bytes 262144 | tf_op jit(solution)/shard_map/all_to_all | solution.py:314
  72.9 8.9 %all-to-all-start.2 = ((f32[4,4,8,128]{3,2,1,0:T(8,128)}), f32[4,4,8,128]{3,2,1,0:T(8,128)S(1)}, u32[]{:S(2)}, u32[]{:S(2)}) async-start(f32[4,4,8,128]{3,2,1,0:T(8,128)} %get-tuple-element.32), calls=%async_computation.2 | async-start | bytes 131072 | tf_op jit(solution)/shard_map/all_to_all | solution.py:314
  107.5 17.8 %collective-permute-start.24 = (f32[2,128]{1,0:T(2,128)S(1)}, f32[2,128]{1,0:T(2,128)S(1)}, u32[]{:S(2)}, u32[]{:S(2)}) collective-permute-start(f32[2,128]{1,0:T(2,128)S(1)} %slice.33), channel_id=1, source_target_pairs={{0,128},{128,0},{1,129},{129,1},{2,130},{130,2},{3,131},{131,3},{4... | collective-permute-start | bytes 3080 | tf_op jit(solution)/shard_map/ppermute | solution.py:450
  107.5 13.8 %collective-permute-start.21 = (f32[192,256]{1,0:T(8,128)}, f32[192,256]{1,0:T(8,128)S(1)}, u32[]{:S(2)}, u32[]{:S(2)}) collective-permute-start(f32[192,256]{1,0:T(8,128)} %get-tuple-element.51), channel_id=1, source_target_pairs={{0,112},{16,0},{32,16},{48,32},{64,48},{80,64},{96,80},{112,96},{1... | collective-permute-start | bytes 589832 | tf_op jit(solution)/shard_map/ppermute | solution.py:310
  110.8 9.6 %collective-permute-start.13 = (f32[128,512]{1,0:T(8,128)S(1)}, f32[128,512]{1,0:T(8,128)S(1)}, u32[]{:S(2)}, u32[]{:S(2)}) collective-permute-start(f32[128,512]{1,0:T(8,128)S(1)} %get-tuple-element.57), channel_id=1, source_target_pairs={{0,4},{4,8},{8,12},{12,0},{1,5},{5,9},{9,13},{13,1},{2,6},{6,10},{... | collective-permute-start | bytes 786440 | tf_op jit(solution)/shard_map/ppermute | solution.py:310
  113.3 8.0 %collective-permute-start.18 = (f32[192,256]{1,0:T(8,128)S(1)}, f32[192,256]{1,0:T(8,128)S(1)}, u32[]{:S(2)}, u32[]{:S(2)}) collective-permute-start(f32[192,256]{1,0:T(8,128)S(1)} %bitcast_add_fusion.4), channel_id=1, source_target_pairs={{0,16},{16,32},{32,48},{48,64},{64,80},{80,96},{96,112},{112,0},{1... | collective-permute-start | bytes 589832 | tf_op jit(solution)/shard_map/ppermute | solution.py:310
  113.5 48.4 %collective-permute-start.16 = (f32[128,1024]{1,0:T(8,128)S(1)}, f32[128,1024]{1,0:T(8,128)S(1)}, u32[]{:S(2)}, u32[]{:S(2)}) collective-permute-start(f32[128,1024]{1,0:T(8,128)S(1)} %pad_maximum_fusion.1), channel_id=1, source_target_pairs={{0,12},{4,0},{8,4},{12,8},{1,13},{5,1},{9,5},{13,9},{2,14},{6,2},{... | collective-permute-start | bytes 1572872 | tf_op jit(solution)/shard_map/ppermute | solution.py:310
  121.3 40.6 %collective-permute-start.14 = (f32[128,1024]{1,0:T(8,128)}, f32[128,1024]{1,0:T(8,128)S(1)}, u32[]{:S(2)}, u32[]{:S(2)}) collective-permute-start(f32[128,1024]{1,0:T(8,128)} %pad_maximum_fusion), channel_id=1, source_target_pairs={{0,4},{4,8},{8,12},{12,0},{1,5},{5,9},{9,13},{13,1},{2,6},{6,10},{... | collective-permute-start | bytes 1572872 | tf_op jit(solution)/shard_map/ppermute | solution.py:310
  122.1 35.0 %collective-permute-start.19 = (f32[192,256]{1,0:T(8,128)}, f32[192,256]{1,0:T(8,128)S(1)}, u32[]{:S(2)}, u32[]{:S(2)}) collective-permute-start(f32[192,256]{1,0:T(8,128)} %get-tuple-element.50), channel_id=1, source_target_pairs={{0,16},{16,32},{32,48},{48,64},{64,80},{80,96},{96,112},{112,0},{1... | collective-permute-start | bytes 589832 | tf_op jit(solution)/shard_map/ppermute | solution.py:310
  122.1 35.0 %collective-permute-start.22 = (f32[192,256]{1,0:T(8,128)S(1)}, f32[192,256]{1,0:T(8,128)}, u32[]{:S(2)}, u32[]{:S(2)}) collective-permute-start(f32[192,256]{1,0:T(8,128)S(1)} %get-tuple-element.49), channel_id=1, source_target_pairs={{0,112},{16,0},{32,16},{48,32},{64,48},{80,64},{96,80},{112,96},{1... | collective-permute-start | bytes 589832 | tf_op jit(solution)/shard_map/ppermute | solution.py:310
  143.3 13.7 %all-to-all-start.6 = ((f32[8,2,128]{2,1,0:T(2,128)}), f32[8,2,128]{2,1,0:T(2,128)S(1)}, u32[]{:S(2)}, u32[]{:S(2)}) async-start(f32[8,2,128]{2,1,0:T(2,128)} %broadcast_in_dim.74), calls=%async_computation.6 | async-start | bytes 16384 | tf_op jit(solution)/shard_map/all_to_all | solution.py:314
  158.7 13.0 %collective-permute-start.20 = (f32[192,256]{1,0:T(8,128)}, f32[192,256]{1,0:T(8,128)S(1)}, u32[]{:S(2)}, u32[]{:S(2)}) collective-permute-start(f32[192,256]{1,0:T(8,128)} %get-tuple-element.48), channel_id=1, source_target_pairs={{0,16},{16,32},{32,48},{48,64},{64,80},{80,96},{96,112},{112,0},{1... | collective-permute-start | bytes 589832 | tf_op jit(solution)/shard_map/ppermute | solution.py:310
  159.3 12.3 %collective-permute-start.23 = (f32[192,256]{1,0:T(8,128)S(1)}, f32[192,256]{1,0:T(8,128)S(1)}, u32[]{:S(2)}, u32[]{:S(2)}) collective-permute-start(f32[192,256]{1,0:T(8,128)S(1)} %get-tuple-element.47), channel_id=1, source_target_pairs={{0,112},{16,0},{32,16},{48,32},{64,48},{80,64},{96,80},{112,96},{1... | collective-permute-start | bytes 589832 | tf_op jit(solution)/shard_map/ppermute | solution.py:310
  165.7 10.1 %all-to-all-start.3 = ((bf16[4,32,1024]{2,1,0:T(8,128)(2,1)}), bf16[4,32,1024]{2,1,0:T(8,128)(2,1)S(1)}, u32[]{:S(2)}, u32[]{:S(2)}) async-start(bf16[4,32,1024]{2,1,0:T(8,128)(2,1)} %bitcast.51), calls=%async_computation.3 | async-start | bytes 524288 | tf_op jit(solution)/shard_map/all_to_all | solution.py:314
  (33 other events, 317.5 us)
